TPU v7x, 32 devices: a whole 2x2x4 slice. The times are simulated.
32 devices in a mesh: rx: 4 (over x, core), ry: 8 (over z, y).
Axes of the slice: x: 2, y: 2, z: 4, core: 2. Of those that a mesh axis runs over, the one named last changes fastest.
Arguments:
- liquid_share: float32 [1024, 5, 640], P(('rx', 'ry')), may hold values from 0 to 1
- thermal_field: float32 [1024, 5, 640], P(('rx', 'ry')), may hold values from -6 to 6
- destination_slab_line: int32 [32, 8, 4], P(('rx', 'ry')), may hold values from 0 to 128, as said below
Outputs:
- image: float32 [4, 4, 32, 640], P(None, None, ('rx', 'ry'))
Inputs may be any that keep to these rules, and one draw needn't show every extreme that they name: `destination_slab_line`: live rows named for one receiving device are distinct. In every draw, in each rx row, some receiving device gets a live brick in all 32 of its slots; the others get between 8 and 32 live bricks.
All inputs are finite; a program needn't handle non-finite values.
Results may differ from a plain program's by a relative error of at most 0.0003.
Values sent between devices are 32-bit elements; how exact they have to be, the bound alone decides.
A program may use at most 128 MiB of HBM per device.

v0:
```python
import jax
import jax.numpy as jnp
from jax import lax
from jax.sharding import PartitionSpec as P

ROWS_DEV = 4


OPACITY = 12.0


def with_halo(array, sides, width):
    for axis, dim in sides:
        size, length = (lax.axis_size(axis), array.shape[dim])
        up = [(i, (i + 1) % size) for i in range(size - 1)]
        down = [(j, i) for i, j in up]
        last = lax.slice_in_dim(array, length - width, length, axis=dim)
        first = lax.slice_in_dim(array, 0, width, axis=dim)
        before = lax.ppermute(last, axis, up)
        after = lax.ppermute(first, axis, down)
        array = jnp.concatenate([before, array, after], axis=dim)
    return array


def swapped(array, axis, stride):
    return lax.ppermute(array, axis, [(i, i ^ 1 << stride) for i in range(lax.axis_size(axis))])


def along_depth(field):
    return 0.25 * field[..., :-2, :, :] + 0.5 * field[..., 1:-1, :, :] + 0.25 * field[..., 2:, :, :]


def along_plane(field):
    leading = [(0, 0)] * (field.ndim - 2)
    padded = jnp.pad(field, leading + [(1, 1), (0, 0)])
    field = 0.25 * padded[..., :-2, :] + 0.5 * padded[..., 1:-1, :] + 0.25 * padded[..., 2:, :]
    padded = jnp.pad(field, leading + [(0, 0), (1, 1)])
    return 0.25 * padded[..., :-2] + 0.5 * padded[..., 1:-1] + 0.25 * padded[..., 2:]


def render_slab(melt_ext, temp_inner, total_depth):
    inner = melt_ext[1:-1]
    grad_z = 0.5 * (melt_ext[2:] - melt_ext[:-2])
    padded = jnp.pad(inner, ((0, 0), (1, 1), (0, 0)))
    grad_y = 0.5 * (padded[:, 2:, :] - padded[:, :-2, :])
    padded = jnp.pad(inner, ((0, 0), (0, 0), (1, 1)))
    grad_x = 0.5 * (padded[:, :, 2:] - padded[:, :, :-2])
    facing = (0.48 * grad_z + 0.6 * grad_y + 0.64 * grad_x) / jnp.sqrt(
        grad_z * grad_z + grad_y * grad_y + grad_x * grad_x + 0.01
    )
    shade = 0.3 + 0.7 * jnp.abs(facing)
    alpha = 1.0 - jnp.exp(inner * (-OPACITY / total_depth))
    through = jnp.cumprod(1.0 - alpha, axis=0)
    before = jnp.concatenate([jnp.ones_like(through[:1]), through[:-1]], axis=0)
    weight = before * alpha * shade
    red = jnp.sum(weight * jax.nn.sigmoid(2.0 * temp_inner), axis=0)
    green = jnp.sum(weight * jnp.exp(-temp_inner * temp_inner), axis=0)
    blue = jnp.sum(weight * jax.nn.sigmoid(-2.0 * temp_inner), axis=0)
    return jnp.stack([red, green, blue, through[-1]])


def layer_over(front, back):
    return jnp.concatenate([front[:3] + front[3:] * back[:3], front[3:] * back[3:]], axis=0)


def split_pair(image, my_bit):
    halves = image.shape[2] // 2
    paired = image.reshape(image.shape[0], image.shape[1], halves, 2, image.shape[3])
    lower = paired[:, :, :, 0]
    upper = paired[:, :, :, 1]
    upper_side = my_bit == 1
    return (jnp.where(upper_side, upper, lower), jnp.where(upper_side, lower, upper))


def join_pair(kept_half, partner, my_bit):
    upper_side = my_bit == 1
    front = jnp.where(upper_side, partner, kept_half)
    back = jnp.where(upper_side, kept_half, partner)
    return layer_over(front, back)


def shards(liquid_share, thermal_field, destination_slab_line):
    count_rx = lax.axis_size("rx")
    receiver_row_count = lax.axis_size("ry")
    devices = count_rx * receiver_row_count
    device_layers = liquid_share.shape[1]
    column_indices = liquid_share.shape[2]
    per_partner_slots = liquid_share.shape[0] // receiver_row_count
    rows_total = ROWS_DEV * devices
    total_depth = device_layers * devices
    position = lax.axis_index("rx") * receiver_row_count + lax.axis_index("ry")
    got_melt, got_temp = (
        lax.all_to_all(
            liquid_share.reshape(
                receiver_row_count, per_partner_slots, device_layers, column_indices
            ),
            "ry",
            split_axis=0,
            concat_axis=0,
            tiled=True,
        ),
        lax.all_to_all(
            thermal_field.reshape(
                receiver_row_count, per_partner_slots, device_layers, column_indices
            ),
            "ry",
            split_axis=0,
            concat_axis=0,
            tiled=True,
        ),
    )
    parcels_held = jnp.stack(
        [
            got_melt.reshape(-1, device_layers, column_indices),
            got_temp.reshape(-1, device_layers, column_indices),
        ]
    )
    targets = destination_slab_line.reshape(-1)
    empty = jnp.zeros((2, device_layers, rows_total, column_indices), jnp.float32)
    slab = empty.at[:, :, targets, :].set(jnp.transpose(parcels_held, (0, 2, 1, 3)), mode="drop")
    padded = with_halo(slab, ((("rx", "ry"), 1),), 2)
    smooth = along_depth(padded)
    layer_mask = jnp.ones((device_layers + 2,), jnp.float32)
    layer_mask = layer_mask.at[0].set(jnp.where(position == 0, 0.0, 1.0))
    layer_mask = layer_mask.at[device_layers + 1].set(jnp.where(position == devices - 1, 0.0, 1.0))
    smooth = along_plane(smooth * layer_mask[None, :, None, None])
    melt_ext = smooth[0]
    temp_inner = smooth[1, 1:-1]
    part = render_slab(melt_ext, temp_inner, total_depth)
    image = part.reshape(4, ROWS_DEV, devices, column_indices)
    column_no = lax.axis_index("ry")
    row_no = lax.axis_index("rx")
    for bit_no in range(receiver_row_count.bit_length() - 1):
        my_bit = column_no >> bit_no & 1
        kept_half, sent_half = split_pair(image, my_bit)
        partner = swapped(sent_half, "ry", bit_no)
        image = join_pair(kept_half, partner, my_bit)
    for bit_no in range(count_rx.bit_length() - 1):
        my_bit = row_no >> bit_no & 1
        kept_half, sent_half = split_pair(image, my_bit)
        partner = swapped(sent_half, "rx", bit_no)
        image = join_pair(kept_half, partner, my_bit)
    return image


def solution(mesh):
    return jax.shard_map(
        shards,
        mesh=mesh,
        in_specs=(
            P(("rx", "ry"), None, None),
            P(("rx", "ry"), None, None),
            P(("rx", "ry"), None, None),
        ),
        out_specs=P(None, None, ("rx", "ry"), None),
        check_vma=False,
    )
```

profile of v0, /device:TPU:0, one launch (start us, length us, event | category | flops | bytes accessed | tf_op | source)
XLA Modules:
  0.0 166.8 jit_solution(566431727067678385)
XLA Ops:
  0.0 1.2 reshape.180
  1.2 0.8 copy.177
  2.0 0.0 copy-start.2
  2.0 7.4 %all-to-all-start = ((f32[8,4,5,640]{3,1,2,0:T(4,128)}), f32[8,4,5,640]{3,1,2,0:T(4,128)S(1)}, u32[]{:S(2)}, u32[]{:S(2)}) async-start(f32[8,4,5,640]{3,1,2,0:T(4,128)} %copy.177), calls=%async_computation | async-start | bytes 819200 | tf_op jit(solution)/shard_map/all_to_all | solution.py:93
  9.4 0.0 copy-done.1
  9.4 0.1 reshape.181
  9.5 0.8 copy.179
  10.3 11.1 %all-to-all-done = f32[8,4,5,640]{3,1,2,0:T(4,128)S(1)} async-done(((f32[8,4,5,640]{3,1,2,0:T(4,128)}), f32[8,4,5,640]{3,1,2,0:T(4,128)S(1)}, u32[]{:S(2)}, u32[]{:S(2)}) %all-to-all-start) | async-done | bytes 409632 | tf_op jit(solution)/shard_map/all_to_all | solution.py:93
  21.4 3.6 %all-to-all-start.1 = ((f32[8,4,5,640]{3,1,2,0:T(4,128)}), f32[8,4,5,640]{3,1,2,0:T(4,128)S(1)}, u32[]{:S(2)}, u32[]{:S(2)}) async-start(f32[8,4,5,640]{3,1,2,0:T(4,128)} %copy.179), calls=%async_computation.1 | async-start | bytes 819200 | tf_op jit(solution)/shard_map/all_to_all | solution.py:102
  25.0 0.0 copy-done.2
  25.0 0.1 copy.176
  25.1 0.1 reshape.179
  25.3 0.1 stack_reshape.6
  25.4 11.6 %all-to-all-done.1 = f32[8,4,5,640]{3,1,2,0:T(4,128)S(1)} async-done(((f32[8,4,5,640]{3,1,2,0:T(4,128)}), f32[8,4,5,640]{3,1,2,0:T(4,128)S(1)}, u32[]{:S(2)}, u32[]{:S(2)}) %all-to-all-start.1) | async-done | bytes 409632 | tf_op jit(solution)/shard_map/all_to_all | solution.py:102
  37.1 0.1 stack_reshape.7
  37.2 0.1 maximum_bitcast_fusion
  37.3 0.6 copy.181
  38.0 2.5 %broadcast_in_dim.2 = f32[2,5,128,640]{3,0,2,1:T(2,128)} broadcast(f32[]{:T(128)} %constant.90.clone.1), dimensions={} | broadcast | bytes 3276804 | tf_op jit(solution)/shard_map/broadcast_in_dim | solution.py:119
  40.5 4.4 %scatter_fusion = f32[2,5,128,640]{3,0,2,1:T(2,128)} fusion(f32[2,5,128,640]{3,0,2,1:T(2,128)} %broadcast_in_dim.2, s32[32]{0:T(128)S(1)} %fusion.40, f32[32,2,5,640]{3,1,2,0:T(2,128)S(1)} %copy.181), kind=kCustom, calls=%fused_computation | custom fusion | bytes 2457728 | tf_op jit(solution)/shard_map/scatter | solution.py:120
  44.9 2.2 %copy.182 = f32[2,5,128,640]{3,2,1,0:T(8,128)S(1)} copy(f32[2,5,128,640]{3,0,2,1:T(2,128)} %scatter_fusion) | data formatting | bytes 6553600 | tf_op jit(solution)/shard_map/scatter | solution.py:120
  47.2 1.7 %fusion.43 = (f32[2,2,128,640]{3,2,1,0:T(8,128)}, f32[2,2,128,640]{3,2,1,0:T(8,128)}) fusion(f32[2,5,128,640]{3,2,1,0:T(8,128)S(1)} %copy.182), kind=kLoop, calls=%fused_computation.112 | loop fusion | bytes 5242880 | tf_op jit(solution)/shard_map/slice | solution.py:17
  48.8 4.6 %collective-permute-start = (f32[2,2,128,640]{3,2,1,0:T(8,128)}, f32[2,2,128,640]{3,2,1,0:T(8,128)}, u32[]{:S(2)}, u32[]{:S(2)}) collective-permute-start(f32[2,2,128,640]{3,2,1,0:T(8,128)} %get-tuple-element.32), channel_id=1, source_target_pairs={{0,1},{1,2},{2,3},{3,4},{4,5},{5,6},{6,7},{7,8},{8,9},{9,10},{10,1... | collective-permute-start | bytes 3932168 | tf_op jit(solution)/shard_map/ppermute | solution.py:19
  53.5 1.5 collective-permute-start.1
  55.0 52.9 %collective-permute-done = f32[2,2,128,640]{3,2,1,0:T(8,128)} collective-permute-done((f32[2,2,128,640]{3,2,1,0:T(8,128)}, f32[2,2,128,640]{3,2,1,0:T(8,128)}, u32[]{:S(2)}, u32[]{:S(2)}) %collective-permute-start) | collective-permute-done | bytes 1310752 | tf_op jit(solution)/shard_map/ppermute | solution.py:19
  107.9 0.0 collective-permute-done.1
  107.9 2.6 %fusion.11 = f32[2,7,128,640]{3,2,1,0:T(8,128)S(1)} fusion(f32[2,2,128,640]{3,2,1,0:T(8,128)} %collective-permute-done.1, f32[2,5,128,640]{3,2,1,0:T(8,128)S(1)} %copy.182, f32[2,2,128,640]{3,2,1,0:T(8,128)} %collective-permute-done, f32[7]{0:T(128)S(1)} %constant_dynamic-update-slice_fusion.4), kind=kLoop, calls=%fused_computation.17 | loop fusion | flops 11468800 | bytes 10485788 | tf_op jit(solution)/shard_map/mul | solution.py:126
  110.5 1.3 fusion.2
  111.8 2.4 %fusion.6 = f32[2,7,128,640]{3,2,1,0:T(8,128)S(1)} fusion(f32[2,7,128,640]{3,2,1,0:T(8,128)S(1)} %fusion.2), kind=kLoop, calls=%fused_computation.11 | loop fusion | flops 5734400 | bytes 9175040 | tf_op jit(solution)/shard_map/add | solution.py:38
  114.3 0.4 fusion.26
  114.7 0.0 copy-start
  114.7 0.1 slice_bitcast_fusion.1
  114.8 0.1 slice.231
  114.9 1.0 copy-done
  115.9 3.1 %multiply_reduce_fusion = (f32[128,640]{1,0:T(8,128)S(1)}, f32[128,640]{1,0:T(8,128)S(1)}, f32[128,640]{1,0:T(8,128)S(1)}) fusion(f32[2,7,128,640]{3,2,1,0:T(8,128)S(1)} %fusion.6, f32[5,128,640]{2,1,0:T(8,128)S(1)} %slice_bitcast_fusion.1, f32[4,128,640]{2,1,0:T(8,128)S(1)} %slice.231), kind=kLoop, calls=%fused_computation.45 | loop fusion | flops 16547840 | bytes 8847360 | tf_op jit(solution)/shard_map/reduce_sum | solution.py:58
  119.1 0.0 slice-start
  119.1 0.2 stack.18
  119.3 0.2 stack.19
  119.5 0.2 stack.20
  119.7 0.3 slice-done
  120.0 0.2 stack.21
  120.2 0.1 constant_dynamic-update-slice_fusion.2
  120.3 0.1 constant_dynamic-update-slice_fusion.1
  120.4 0.1 constant_dynamic-update-slice_fusion
  120.5 1.2 broadcast_select_fusion
  121.7 0.1 fusion.30
  121.8 2.5 %collective-permute-start.2 = (f32[4,4,16,640]{3,2,1,0:T(8,128)S(1)}, f32[4,4,16,640]{3,2,1,0:T(8,128)S(1)}, u32[]{:S(2)}, u32[]{:S(2)}) collective-permute-start(f32[4,4,16,640]{3,2,1,0:T(8,128)S(1)} %fusion.30), channel_id=1, source_target_pairs={{0,1},{1,0},{2,3},{3,2},{4,5},{5,4},{6,7},{7,6},{8,9},{9,8},{10,11... | collective-permute-start | bytes 1966088 | tf_op jit(solution)/shard_map/ppermute | solution.py:26
  124.4 12.9 %collective-permute-done.2 = f32[4,4,16,640]{3,2,1,0:T(8,128)S(1)} collective-permute-done((f32[4,4,16,640]{3,2,1,0:T(8,128)S(1)}, f32[4,4,16,640]{3,2,1,0:T(8,128)S(1)}, u32[]{:S(2)}, u32[]{:S(2)}) %collective-permute-start.2) | collective-permute-done | bytes 655392 | tf_op jit(solution)/shard_map/ppermute | solution.py:26
  137.2 0.1 bitcast_select_fusion.1
  137.4 0.1 fusion.31
  137.5 0.3 copy.191
  137.8 0.1 fusion.32
  137.9 3.6 %collective-permute-start.3 = (f32[4,4,8,640]{3,1,2,0:T(4,128)S(1)}, f32[4,4,8,640]{3,1,2,0:T(4,128)S(1)}, u32[]{:S(2)}, u32[]{:S(2)}) collective-permute-start(f32[4,4,8,640]{3,1,2,0:T(4,128)S(1)} %fusion.32), channel_id=1, source_target_pairs={{0,2},{1,3},{2,0},{3,1},{4,6},{5,7},{6,4},{7,5},{8,10},{9,11},{10,... | collective-permute-start | bytes 983048 | tf_op jit(solution)/shard_map/ppermute | solution.py:26
  141.4 7.0 %collective-permute-done.3 = f32[4,4,8,640]{3,1,2,0:T(4,128)S(1)} collective-permute-done((f32[4,4,8,640]{3,1,2,0:T(4,128)S(1)}, f32[4,4,8,640]{3,1,2,0:T(4,128)S(1)}, u32[]{:S(2)}, u32[]{:S(2)}) %collective-permute-start.3) | collective-permute-done | bytes 327712 | tf_op jit(solution)/shard_map/ppermute | solution.py:26
  148.5 0.1 bitcast_select_fusion.4
  148.7 0.1 fusion.33
  148.8 0.1 pad_maximum_fusion.3
  148.9 2.8 %collective-permute-start.4 = (f32[4,4,4,640]{3,1,2,0:T(4,128)S(1)}, f32[4,4,4,640]{3,1,2,0:T(4,128)S(1)}, u32[]{:S(2)}, u32[]{:S(2)}) collective-permute-start(f32[4,4,4,640]{3,1,2,0:T(4,128)S(1)} %fusion.34), channel_id=1, source_target_pairs={{0,4},{1,5},{2,6},{3,7},{4,0},{5,1},{6,2},{7,3},{8,12},{9,13},{10,... | collective-permute-start | bytes 491528 | tf_op jit(solution)/shard_map/ppermute | solution.py:26
  151.7 6.3 %collective-permute-done.4 = f32[4,4,4,640]{3,1,2,0:T(4,128)S(1)} collective-permute-done((f32[4,4,4,640]{3,1,2,0:T(4,128)S(1)}, f32[4,4,4,640]{3,1,2,0:T(4,128)S(1)}, u32[]{:S(2)}, u32[]{:S(2)}) %collective-permute-start.4) | collective-permute-done | bytes 163872 | tf_op jit(solution)/shard_map/ppermute | solution.py:26
  158.0 0.1 bitcast_select_fusion.8
  158.2 0.1 collective-permute-start.5
  158.3 1.3 collective-permute-done.5
  159.7 4.4 %collective-permute-start.6 = (f32[4,4,1,640]{3,1,0,2:T(4,128)S(1)}, f32[4,4,1,640]{3,1,0,2:T(4,128)S(1)}, u32[]{:S(2)}, u32[]{:S(2)}) collective-permute-start(f32[4,4,1,640]{3,1,0,2:T(4,128)S(1)} %fusion.38), channel_id=1, source_target_pairs={{0,16},{8,24},{16,0},{24,8},{1,17},{9,25},{17,1},{25,9},{2,18},{10... | collective-permute-start | bytes 122888 | tf_op jit(solution)/shard_map/ppermute | solution.py:26
  164.1 2.0 %collective-permute-done.6 = f32[4,4,1,640]{3,1,0,2:T(4,128)S(1)} collective-permute-done((f32[4,4,1,640]{3,1,0,2:T(4,128)S(1)}, f32[4,4,1,640]{3,1,0,2:T(4,128)S(1)}, u32[]{:S(2)}, u32[]{:S(2)}) %collective-permute-start.6) | collective-permute-done | bytes 40992 | tf_op jit(solution)/shard_map/ppermute | solution.py:26
  166.2 0.7 copy.208
  (24 shorter events, 0.6 us)
Async XLA Ops:
  0.0 9.4 %copy-start.1 = (f32[32,5,640]{2,0,1:T(8,128)S(1)}, f32[32,5,640]{2,0,1:T(8,128)}, u32[]{:S(2)}) copy-start(f32[32,5,640]{2,0,1:T(8,128)} %param.8) | copy-start | bytes 1228804
  2.0 23.1 %copy-start.2 = (s32[1,8,4]{1,2,0:T(4,128)S(1)}, s32[1,8,4]{1,2,0:T(4,128)}, u32[]{:S(2)}) copy-start(s32[1,8,4]{1,2,0:T(4,128)} %param.9) | copy-start | bytes 388
  2.0 19.4 %all-to-all-start = ((f32[8,4,5,640]{3,1,2,0:T(4,128)}), f32[8,4,5,640]{3,1,2,0:T(4,128)S(1)}, u32[]{:S(2)}, u32[]{:S(2)}) async-start(f32[8,4,5,640]{3,1,2,0:T(4,128)} %copy.177), calls=%async_computation | async-start | bytes 819200 | tf_op jit(solution)/shard_map/all_to_all | solution.py:93
  21.4 15.6 %all-to-all-start.1 = ((f32[8,4,5,640]{3,1,2,0:T(4,128)}), f32[8,4,5,640]{3,1,2,0:T(4,128)S(1)}, u32[]{:S(2)}, u32[]{:S(2)}) async-start(f32[8,4,5,640]{3,1,2,0:T(4,128)} %copy.179), calls=%async_computation.1 | async-start | bytes 819200 | tf_op jit(solution)/shard_map/all_to_all | solution.py:102
  48.8 59.1 %collective-permute-start = (f32[2,2,128,640]{3,2,1,0:T(8,128)}, f32[2,2,128,640]{3,2,1,0:T(8,128)}, u32[]{:S(2)}, u32[]{:S(2)}) collective-permute-start(f32[2,2,128,640]{3,2,1,0:T(8,128)} %get-tuple-element.32), channel_id=1, source_target_pairs={{0,1},{1,2},{2,3},{3,4},{4,5},{5,6},{6,7},{7,8},{8,9},{9,10},{10,1... | collective-permute-start | bytes 3932168 | tf_op jit(solution)/shard_map/ppermute | solution.py:19
  53.5 54.4 %collective-permute-start.1 = (f32[2,2,128,640]{3,2,1,0:T(8,128)}, f32[2,2,128,640]{3,2,1,0:T(8,128)}, u32[]{:S(2)}, u32[]{:S(2)}) collective-permute-start(f32[2,2,128,640]{3,2,1,0:T(8,128)} %get-tuple-element.33), channel_id=1, source_target_pairs={{1,0},{2,1},{3,2},{4,3},{5,4},{6,5},{7,6},{8,7},{9,8},{10,9},{11,1... | collective-permute-start | bytes 3932168 | tf_op jit(solution)/shard_map/ppermute | solution.py:20
  114.7 1.2 copy-start
  119.1 1.0 slice-start
  121.8 15.4 %collective-permute-start.2 = (f32[4,4,16,640]{3,2,1,0:T(8,128)S(1)}, f32[4,4,16,640]{3,2,1,0:T(8,128)S(1)}, u32[]{:S(2)}, u32[]{:S(2)}) collective-permute-start(f32[4,4,16,640]{3,2,1,0:T(8,128)S(1)} %fusion.30), channel_id=1, source_target_pairs={{0,1},{1,0},{2,3},{3,2},{4,5},{5,4},{6,7},{7,6},{8,9},{9,8},{10,11... | collective-permute-start | bytes 1966088 | tf_op jit(solution)/shard_map/ppermute | solution.py:26
  137.9 10.6 %collective-permute-start.3 = (f32[4,4,8,640]{3,1,2,0:T(4,128)S(1)}, f32[4,4,8,640]{3,1,2,0:T(4,128)S(1)}, u32[]{:S(2)}, u32[]{:S(2)}) collective-permute-start(f32[4,4,8,640]{3,1,2,0:T(4,128)S(1)} %fusion.32), channel_id=1, source_target_pairs={{0,2},{1,3},{2,0},{3,1},{4,6},{5,7},{6,4},{7,5},{8,10},{9,11},{10,... | collective-permute-start | bytes 983048 | tf_op jit(solution)/shard_map/ppermute | solution.py:26
  148.9 9.1 %collective-permute-start.4 = (f32[4,4,4,640]{3,1,2,0:T(4,128)S(1)}, f32[4,4,4,640]{3,1,2,0:T(4,128)S(1)}, u32[]{:S(2)}, u32[]{:S(2)}) collective-permute-start(f32[4,4,4,640]{3,1,2,0:T(4,128)S(1)} %fusion.34), channel_id=1, source_target_pairs={{0,4},{1,5},{2,6},{3,7},{4,0},{5,1},{6,2},{7,3},{8,12},{9,13},{10,... | collective-permute-start | bytes 491528 | tf_op jit(solution)/shard_map/ppermute | solution.py:26
  158.2 1.3 collective-permute-start.5
  159.7 6.4 %collective-permute-start.6 = (f32[4,4,1,640]{3,1,0,2:T(4,128)S(1)}, f32[4,4,1,640]{3,1,0,2:T(4,128)S(1)}, u32[]{:S(2)}, u32[]{:S(2)}) collective-permute-start(f32[4,4,1,640]{3,1,0,2:T(4,128)S(1)} %fusion.38), channel_id=1, source_target_pairs={{0,16},{8,24},{16,0},{24,8},{1,17},{9,25},{17,1},{25,9},{2,18},{10... | collective-permute-start | bytes 122888 | tf_op jit(solution)/shard_map/ppermute | solution.py:26
where the time goes:
time: 168 us; the launch traced here: 167 us
  waiting for transfers between devices  105 us (62%)
  starting transfers between devices  30.6 us (18%)
  local copies, waits for them, and re-layouts  18.4 us (11%)
  other arithmetic  12.3 us (7%)
    ppermute x1, waiting for transfers between devices, with_halo(): before = lax.ppermute(last, axis, up)  52.9 us
    ppermute x5, waiting for transfers between devices, swapped(): lax.ppermute(array, axis, [(i, i ^ 1 << stride) for i in range(lax.axis_s...  29.4 us
    ppermute x5, starting transfers between devices, swapped(): lax.ppermute(array, axis, [(i, i ^ 1 << stride) for i in range(lax.axis_s...  13.4 us
    all_to_all x1, waiting for transfers between devices, shards(): lax.all_to_all(thermal_field.reshape(receiver_row_count, per_partner_slot...  11.6 us
    all_to_all x1, waiting for transfers between devices, shards(): lax.all_to_all(liquid_share.reshape(receiver_row_count, per_partner_slots...  11.1 us
    all_to_all x1, starting transfers between devices, shards(): lax.all_to_all(liquid_share.reshape(receiver_row_count, per_partner_slots...  7.41 us
    scatter x2, local copies, waits for them, and re-layouts, shards(): empty.at[:, :, targets, :]  6.67 us
    ppermute x1, starting transfers between devices, with_halo(): before = lax.ppermute(last, axis, up)  4.64 us
  transfers between devices with their start and end apart: 9, of which 8 were waited for; matrix products, arithmetic and copies ran while one was open for 1% of the time, Pallas kernels for 0%

commit v1 on v0

v1 whole, which is shorter than its diff:
```python
import functools

import jax
import jax.numpy as jnp
from jax import lax
from jax.experimental import pallas as pl
from jax.experimental.pallas import tpu as pltpu
from jax.sharding import PartitionSpec as P

ROWS_DEV = 4
OPACITY = 12.0
MESH = pl.DeviceIdType.MESH
F32 = jnp.float32
BF16 = jnp.bfloat16


def kernel(
    n_rx, n_ry, cap, layers, width,
    melt_ref, temp_ref, t_ref, out_ref,
    send, recv, before, after, lines,
    rhs_b, rhs_d, rhs_e, rhs_p, rhs_n, weights,
    sm, st, gy, gx, img, cin, send2, parts,
    a_send, a_recv, hp_send, hp_recv, hn_send, hn_recv, t_send, t_recv,
    c_send, c_recv, d_send, d_recv,
):
    n_dev = n_rx * n_ry
    rows = ROWS_DEV * n_dev
    half_rows = rows // 2
    n_low = n_dev // 2
    k0 = n_ry * 2 * cap
    r, j = lax.axis_index("rx"), lax.axis_index("ry")
    me = r * n_ry + j
    core = r % 2

    def worker(rr, dd):
        return ((rr // 2) * 2 + dd % 2, (dd // 2) * 2 + rr % 2)

    def worker_of(slab):
        return worker(slab // n_ry, slab % n_ry)

    src_r, slab_d = worker(r, j)
    slab = src_r * n_ry + slab_d
    own_block = core == j % 2
    has_prev, has_next = slab > 0, slab < n_dev - 1

    barrier = pltpu.get_barrier_semaphore()

    def greet(i, c):
        other = (me + i) % n_dev
        pl.semaphore_signal(barrier, inc=1, device_id=(other // n_ry, other % n_ry), device_id_type=MESH)
        return c

    lax.fori_loop(1, n_dev, greet, 0)

    for field, ref in enumerate((melt_ref, temp_ref)):
        for b in range(n_ry * cap):
            d = b // cap
            send[d * layers : (d + 1) * layers, field * cap + b % cap, :] = ref[b]

    @pl.when(jnp.logical_not(has_prev))
    def _():
        before[...] = jnp.zeros_like(before)
        lines[1] = jnp.full_like(lines[1], 1e4)

    @pl.when(jnp.logical_not(has_next))
    def _():
        after[...] = jnp.zeros_like(after)
        lines[2] = jnp.full_like(lines[2], 1e4)

    pl.semaphore_wait(barrier, n_dev - 1)

    def line_copy(which, target):
        return pltpu.make_async_remote_copy(
            t_ref, lines.at[which], t_send.at[which], t_recv.at[which],
            device_id=target, device_id_type=MESH)

    @pl.when(me < n_dev - 1)
    def _():
        line_copy(1, worker_of(me + 1)).start()

    @pl.when(me > 0)
    def _():
        line_copy(2, worker_of(me - 1)).start()

    @pl.when(own_block)
    def _():
        lines[0] = t_ref[...]

    @pl.when(jnp.logical_not(own_block))
    def _():
        line_copy(0, worker(r, j)).start()

    def brick_copy(i):
        d = (j + i) % n_ry
        return pltpu.make_async_remote_copy(
            send.at[pl.ds(d * layers, layers)], recv.at[j], a_send.at[i], a_recv.at[j],
            device_id=worker(r, d), device_id_type=MESH)

    for i in range(1, n_ry):
        brick_copy(i).start()

    @pl.when(jnp.logical_not(own_block))
    def _():
        brick_copy(0).start()

    @pl.when(own_block)
    def _():
        recv[j] = send[pl.ds(j * layers, layers)]

    @pl.when(jnp.logical_not(own_block))
    def _():
        line_copy(0, worker(r, j)).wait_recv()

    @pl.when(has_prev)
    def _():
        line_copy(1, worker(r, j)).wait_recv()

    @pl.when(has_next)
    def _():
        line_copy(2, worker(r, j)).wait_recv()

    p = lax.broadcasted_iota(jnp.int32, (rows, 2 * k0), 0)
    lane = lax.broadcasted_iota(jnp.int32, (rows, 2 * k0), 1)
    log_ry, log_low = n_ry.bit_length() - 1, n_low.bit_length() - 1
    other_half = jnp.where(p < half_rows, 1, 0)
    side = jnp.where(other_half == 1, 1 - core, core)
    part_a = (p >> log_low) & (ROWS_DEV - 1)
    low = p & (n_low - 1)
    k = ((low >> log_ry) << (log_ry + 1)) + side * n_ry + (low & (n_ry - 1))
    q = (part_a * n_dev + k).astype(F32)
    is_melt = (lane & cap) == 0

    def hat(v):
        return jnp.maximum(0.5 - 0.25 * jnp.abs(v), 0.0)

    for which in range(3):
        u = lines[which, 0:1, :] - q
        s = hat(u)
        g = 0.5 * (jnp.where(q < rows - 1, hat(u - 1.0), 0.0) - jnp.where(q > 0, hat(u + 1.0), 0.0))
        weights[which, 0:rows] = jnp.where(is_melt, s, 0.0).astype(BF16)
        weights[which, rows : 2 * rows] = jnp.where(is_melt, 0.0, s).astype(BF16)
        weights[which, 2 * rows : 3 * rows] = jnp.where(is_melt, g, 0.0).astype(BF16)

    col = lax.broadcasted_iota(jnp.int32, (4 * cap, width), 1)

    def from_left(x):
        return jnp.where(col == 0, 0.0, pltpu.roll(x, 1, 1))

    def from_right(x):
        return jnp.where(col == width - 1, 0.0, pltpu.roll(x, width - 1, 1))

    def smooth_x(x):
        return 0.5 * x + 0.25 * (from_left(x) + from_right(x))

    def diff_x(x):
        return 0.5 * (from_right(x) - from_left(x))

    def put(ref, index, first, x):
        hi = x.astype(BF16)
        ref[index, first : first + 4 * cap] = hi
        ref[index, k0 + first : k0 + first + 4 * cap] = (x - hi.astype(F32)).astype(BF16)

    def rows_of(ref, pair, layer):
        return ref[2 * pair : 2 * pair + 2, layer].reshape(4 * cap, width)

    def before_copy(jj):
        return pltpu.make_async_remote_copy(
            recv.at[jj, pl.ds(layers - 2, 2)], before.at[jj], hp_send.at[jj], hp_recv.at[jj],
            device_id=worker_of((slab + 1) % n_dev), device_id_type=MESH)

    def after_copy(jj):
        return pltpu.make_async_remote_copy(
            recv.at[jj, pl.ds(0, 2)], after.at[jj], hn_send.at[jj], hn_recv.at[jj],
            device_id=worker_of((slab + n_dev - 1) % n_dev), device_id_type=MESH)

    def brick_wait(jj):
        pltpu.make_async_remote_copy(
            send.at[pl.ds(0, layers)], recv.at[jj], a_send.at[0], a_recv.at[jj],
            device_id=worker(r, j), device_id_type=MESH).wait_recv()

    for pair in range(n_ry // 2):
        for jj in (2 * pair, 2 * pair + 1):
            @pl.when(jnp.logical_not(jnp.logical_and(own_block, j == jj)))
            def _():
                brick_wait(jj)

            @pl.when(has_next)
            def _():
                before_copy(jj).start()

            @pl.when(has_prev)
            def _():
                after_copy(jj).start()

        first = pair * 4 * cap
        xs = [smooth_x(rows_of(recv, pair, z)) for z in range(layers)]
        for z in range(layers):
            b = 0.5 * xs[z]
            if z > 0:
                b = b + 0.25 * xs[z - 1]
            if z < layers - 1:
                b = b + 0.25 * xs[z + 1]
            put(rhs_b, z, first, b)
            put(rhs_d, z, first, diff_x(b))
        put(rhs_e, 0, first, 0.25 * xs[0])
        put(rhs_e, 1, first, 0.25 * xs[layers - 1])

    def dot(which, lo, hi, rhs):
        return jnp.dot(weights[which, lo * rows : hi * rows], rhs, preferred_element_type=F32)

    for z in range(layers):
        res = dot(0, 0, 3, rhs_b[z])
        sm[z + 1] = res[0:rows]
        st[z] = res[rows : 2 * rows]
        gy[z] = res[2 * rows : 3 * rows]
        gx[z] = dot(0, 0, 1, rhs_d[z])
    sm[0] = dot(0, 0, 1, rhs_e[0])
    sm[layers + 1] = dot(0, 0, 1, rhs_e[1])

    for pair in range(n_ry // 2):
        for jj in (2 * pair, 2 * pair + 1):
            @pl.when(has_prev)
            def _():
                before_copy(jj).wait_recv()

            @pl.when(has_next)
            def _():
                after_copy(jj).wait_recv()

        first = pair * 4 * cap
        p3, p4 = (smooth_x(rows_of(before, pair, z)) for z in (0, 1))
        n0, n1 = (smooth_x(rows_of(after, pair, z)) for z in (0, 1))
        put(rhs_p, 0, first, 0.25 * p4)
        put(rhs_p, 1, first, 0.25 * diff_x(p4))
        put(rhs_p, 2, first, 0.25 * p3 + 0.5 * p4)
        put(rhs_n, 0, first, 0.25 * n0)
        put(rhs_n, 1, first, 0.25 * diff_x(n0))
        put(rhs_n, 2, first, 0.25 * n1 + 0.5 * n0)

    for which, rhs, z, edge, present in ((1, rhs_p, 0, 0, has_prev), (2, rhs_n, layers - 1, layers + 1, has_next)):
        res = dot(which, 0, 3, rhs[0])
        sm[z + 1] += res[0:rows]
        st[z] += res[rows : 2 * rows]
        gy[z] += res[2 * rows : 3 * rows]
        gx[z] += dot(which, 0, 1, rhs[1])
        sm[edge] = jnp.where(present, sm[edge] + dot(which, 0, 1, rhs[2]), 0.0)

    decay = -OPACITY / (layers * n_dev)

    def march(half):
        def tile(i, c):
            at = pl.ds(pl.multiple_of(half * half_rows + i * 8, 8), 8)
            through = total = red = green = None
            for z in range(layers):
                s = sm[z + 1, at, :]
                dz = 0.5 * (sm[z + 2, at, :] - sm[z, at, :])
                dy, dx = gy[z, at, :], gx[z, at, :]
                t = st[z, at, :]
                facing = (0.48 * dz + 0.6 * dy + 0.64 * dx) * lax.rsqrt(dz * dz + dy * dy + dx * dx + 0.01)
                shade = 0.3 + 0.7 * jnp.abs(facing)
                kept = jnp.exp(s * decay)
                w = (1.0 - kept) * shade
                if z > 0:
                    w = w * through
                rw = w / (1.0 + jnp.exp(-2.0 * t))
                gw = w * jnp.exp(-t * t)
                if z == 0:
                    through, total, red, green = kept, w, rw, gw
                else:
                    through, total, red, green = through * kept, total + w, red + rw, green + gw
            to = pl.ds(pl.multiple_of(i * 8, 8), 8)
            img[half, 0, to, :] = red
            img[half, 1, to, :] = green
            img[half, 2, to, :] = total - red
            img[half, 3, to, :] = through
            return c

        lax.fori_loop(0, half_rows // 8, tile, 0)

    march(0)
    core_copy = pltpu.make_async_remote_copy(
        img.at[0], cin, c_send, c_recv, device_id=((r // 2) * 2 + 1 - core, j), device_id_type=MESH)
    core_copy.start()
    march(1)
    core_copy.wait_recv()

    front = core == 0

    for a in range(ROWS_DEV):
        for low8 in range(n_low // 8):
            at = slice(a * n_low + low8 * 8, a * n_low + low8 * 8 + 8)
            mine = [img[1, ch, at, :] for ch in range(4)]
            theirs = [cin[ch, at, :] for ch in range(4)]
            ft = jnp.where(front, mine[3], theirs[3])
            for ch in range(4):
                f = jnp.where(front, mine[ch], theirs[ch])
                b = jnp.where(front, theirs[ch], mine[ch])
                value = f + ft * b if ch < 3 else ft * b
                send2[low8 * 8 : low8 * 8 + 8, ch * ROWS_DEV + a, :] = value

    low_me = (r // 2) * n_ry + j
    group = (r // 2) * n_ry + (j % 2) * (n_ry // 2) + j // 2

    def part_copy(i):
        to = (low_me + i) % n_low
        return pltpu.make_async_remote_copy(
            send2.at[to], parts.at[group], d_send.at[i], d_recv.at[group],
            device_id=((to // n_ry) * 2 + core, to % n_ry), device_id_type=MESH)

    for i in range(1, n_low):
        part_copy(i).start()
    parts[group] = send2[low_me]

    color, through = None, None
    for g in range(n_low):
        @pl.when(g != group)
        def _():
            pltpu.make_async_remote_copy(
                send2.at[0], parts.at[g], d_send.at[0], d_recv.at[g],
                device_id=(r, j), device_id_type=MESH).wait_recv()

        value = parts[g]
        c = value[: 3 * ROWS_DEV]
        t = value[3 * ROWS_DEV :]
        if g == 0:
            color, through = c, t
        else:
            color = color + jnp.concatenate([through] * 3, axis=0) * c
            through = through * t
    out_ref[: 3 * ROWS_DEV] = color
    out_ref[3 * ROWS_DEV :] = through

    @pl.when(me < n_dev - 1)
    def _():
        line_copy(1, worker(r, j)).wait_send()

    @pl.when(me > 0)
    def _():
        line_copy(2, worker(r, j)).wait_send()

    @pl.when(jnp.logical_not(own_block))
    def _():
        line_copy(0, worker(r, j)).wait_send()
        brick_copy(0).wait_send()

    for i in range(1, n_ry):
        brick_copy(i).wait_send()
    for jj in range(n_ry):
        @pl.when(has_next)
        def _():
            before_copy(jj).wait_send()

        @pl.when(has_prev)
        def _():
            after_copy(jj).wait_send()

    core_copy.wait_send()
    for i in range(1, n_low):
        part_copy(i).wait_send()


def shards(liquid_share, thermal_field, destination_slab_line):
    n_rx, n_ry = lax.axis_size("rx"), lax.axis_size("ry")
    bricks, layers, width = liquid_share.shape
    cap = bricks // n_ry
    n_dev = n_rx * n_ry
    rows = ROWS_DEV * n_dev
    k0 = n_ry * 2 * cap
    lines = destination_slab_line.reshape(n_ry, 1, cap).astype(F32)
    lines = jnp.where(lines >= rows, 1e4, lines)
    lines = jnp.broadcast_to(lines, (n_ry, 2, cap)).reshape(1, k0)
    lines = jnp.broadcast_to(jnp.concatenate([lines, lines], axis=1), (8, 2 * k0))
    dma = pltpu.SemaphoreType.DMA
    vmem = pltpu.VMEM
    half_rows, n_low = rows // 2, n_dev // 2
    image = pl.pallas_call(
        functools.partial(kernel, n_rx, n_ry, cap, layers, width),
        out_shape=jax.ShapeDtypeStruct((4 * ROWS_DEV, width), F32),
        in_specs=[pl.BlockSpec(memory_space=pltpu.VMEM)] * 3,
        out_specs=pl.BlockSpec(memory_space=pltpu.VMEM),
        scratch_shapes=[
            vmem((n_ry * layers, 2 * cap, width), F32),
            vmem((n_ry, layers, 2 * cap, width), F32),
            vmem((n_ry, 2, 2 * cap, width), F32),
            vmem((n_ry, 2, 2 * cap, width), F32),
            vmem((3, 8, 2 * k0), F32),
            vmem((layers, 2 * k0, width), BF16),
            vmem((layers, 2 * k0, width), BF16),
            vmem((2, 2 * k0, width), BF16),
            vmem((3, 2 * k0, width), BF16),
            vmem((3, 2 * k0, width), BF16),
            vmem((3, 3 * rows, 2 * k0), BF16),
            vmem((layers + 2, rows, width), F32),
            vmem((layers, rows, width), F32),
            vmem((layers, rows, width), F32),
            vmem((layers, rows, width), F32),
            vmem((2, 4, half_rows, width), F32),
            vmem((4, half_rows, width), F32),
            vmem((n_low, 4 * ROWS_DEV, width), F32),
            vmem((n_low, 4 * ROWS_DEV, width), F32),
            dma((n_ry,)), dma((n_ry,)),
            dma((n_ry,)), dma((n_ry,)),
            dma((n_ry,)), dma((n_ry,)),
            dma((3,)), dma((3,)),
            dma, dma,
            dma((n_low,)), dma((n_low,)),
        ],
        compiler_params=pltpu.CompilerParams(
            collective_id=0, has_side_effects=True, vmem_limit_bytes=60 * 1024 * 1024),
    )(liquid_share, thermal_field, lines)
    return image.reshape(4, ROWS_DEV, 1, width)


def solution(mesh):
    return jax.shard_map(
        shards,
        mesh=mesh,
        in_specs=(
            P(("rx", "ry"), None, None),
            P(("rx", "ry"), None, None),
            P(("rx", "ry"), None, None),
        ),
        out_specs=P(None, None, ("rx", "ry"), None),
        check_vma=False,
    )
```

time: 168 us -> 60.6 us (0.36)
  waiting for transfers between devices: 105 us -> 0 us
  Pallas kernels: 0 us -> 53.3 us
  starting transfers between devices: 30.6 us -> 0 us
  local copies, waits for them, and re-layouts: 18.4 us -> 5.49 us
  other arithmetic: 12.3 us -> 0.76 us
    ppermute x7 -> x0, waiting for transfers between devices: 82.4 us -> none  [the longest x1 52.9 us: with_halo(): before = lax.ppermute(last, axis, up)]
    pallas_call x0 -> x1, Pallas kernels: none -> 53.3 us  [shards(): pl.pallas_call(functools.partial(kernel, n_rx, n_ry, cap, layers, width),...]
    all_to_all x2 -> x0, waiting for transfers between devices: 22.7 us -> none  [the longest x1 11.6 us: shards(): lax.all_to_all(thermal_field.reshape(receiver_row_count, per_partner_slot...]
    ppermute x7 -> x0, starting transfers between devices: 19.5 us -> none  [the longest x5 13.4 us: swapped(): lax.ppermute(array, axis, [(i, i ^ 1 << stride) for i in range(lax.axis_s...]
    all_to_all x2 -> x0, starting transfers between devices: 11 us -> none  [the longest x1 7.41 us: shards(): lax.all_to_all(liquid_share.reshape(receiver_row_count, per_partner_slots...]
    scatter x4 -> x0, local copies, waits for them, and re-layouts: 6.69 us -> none  [the longest x2 6.67 us: shards(): empty.at[:, :, targets, :]]
    add x7 -> x0, other arithmetic: 3.97 us -> none  [the longest x1 2.43 us: along_plane(): 0.25 * padded[..., :-2] + 0.5 * padded[..., 1:-1] + 0.25 * padded[..., 2:]]
    reduce_sum x1 -> x0, other arithmetic: 3.13 us -> none  [render_slab(): blue = jnp.sum(weight * jax.nn.sigmoid(-2.0 * temp_inner), axis=0)]
  transfers between devices with their start and end apart: 9 -> 0, of which waited for: 8 -> 0; matrix products, arithmetic and copies ran while one was open for 1% -> 0% of each run, Pallas kernels for 0% -> 0%
where the time goes in v1:
time: 60.6 us; the launch traced here: 59.6 us
  Pallas kernels  53.3 us (88%)
  local copies, waits for them, and re-layouts  5.49 us (9%)
  other arithmetic  0.76 us (1%)
    pallas_call x1, Pallas kernels, shards(): pl.pallas_call(functools.partial(kernel, n_rx, n_ry, cap, layers, width),...  53.3 us
    unnamed x4, local copies, waits for them, and re-layouts  3.27 us
    reshape x1, local copies, waits for them, and re-layouts, shards(): return image.reshape(4, ROWS_DEV, 1, width)  1.43 us

profile of v1, /device:TPU:0, one launch (start us, length us, event | category | flops | bytes accessed | tf_op | source)
XLA Modules:
  0.0 59.6 jit_solution(13161462289307050842)
XLA Ops:
  0.0 0.7 %compare_select_fusion = f32[8,4]{0,1:T(4,128)S(1)} fusion(s32[1,8,4]{1,2,0:T(4,128)} %param.5), kind=kLoop, calls=%fused_computation | loop fusion | flops 96 | bytes 256 | tf_op jit(solution)/shard_map/jit(_where)/select_n | solution.py:370
  0.7 0.1 copy.8
  0.8 0.1 reshape.19
  0.9 0.1 maximum_bitcast_fusion
  0.9 0.6 %broadcast_in_dim.19.t_ref = f32[8,128]{1,0:T(8,128)} broadcast(f32[128]{0:T(128)S(1)} %maximum_bitcast_fusion), dimensions={1} | broadcast | bytes 4608 | tf_op jit(solution)/shard_map/broadcast_in_dim | solution.py:372
  1.6 0.0 copy-start
  1.6 2.2 %copy.9.melt_ref = f32[32,5,640]{2,1,0:T(8,128)} copy(f32[32,5,640]{2,0,1:T(8,128)} %param.3) | data formatting | bytes 819200 | tf_op args[0]
  3.7 0.0 copy-done
  3.7 1.1 %copy.10.temp_ref = f32[32,5,640]{2,1,0:T(8,128)} copy(f32[32,5,640]{2,0,1:T(8,128)S(1)} %copy-done) | data formatting | bytes 819200 | tf_op args[1]
  4.8 53.3 %shard_map.37 = f32[16,640]{1,0:T(8,128)} custom-call(f32[32,5,640]{2,1,0:T(8,128)} %copy.9.melt_ref, f32[32,5,640]{2,1,0:T(8,128)} %copy.10.temp_ref, f32[8,128]{1,0:T(8,128)} %broadcast_in_dim.19.t_ref), custom_call_target="tpu_custom_call" | custom-call | tf_op jit(solution)/shard_map/pallas_call | solution.py:376
  58.1 1.4 %reshape.21 = f32[4,4,1,640]{3,2,1,0:T(1,128)} reshape(f32[16,640]{1,0:T(8,128)} %shard_map.37) | data formatting | bytes 81920 | tf_op jit(solution)/shard_map/reshape | solution.py:411
  (1 shorter events, 0.0 us)
Async XLA Ops:
  1.6 2.2 %copy-start = (f32[32,5,640]{2,0,1:T(8,128)S(1)}, f32[32,5,640]{2,0,1:T(8,128)}, u32[]{:S(2)}) copy-start(f32[32,5,640]{2,0,1:T(8,128)} %param.4) | copy-start | bytes 1228804

commit v2 on v1

--- a/solution.py
+++ b/solution.py
@@ -16,12 +16,12 @@
 
 def kernel(
     n_rx, n_ry, cap, layers, width,
-    melt_ref, temp_ref, t_ref, out_ref,
-    send, recv, before, after, lines,
+    melt_ref, temp_ref, names_ref, out_ref,
+    held, t_ref, send, recv, before, after, lines,
     rhs_b, rhs_d, rhs_e, rhs_p, rhs_n, weights,
     sm, st, gy, gx, img, cin, send2, parts,
     a_send, a_recv, hp_send, hp_recv, hn_send, hn_recv, t_send, t_recv,
-    c_send, c_recv, d_send, d_recv,
+    c_send, c_recv, d_send, d_recv, in_sem,
 ):
     n_dev = n_rx * n_ry
     rows = ROWS_DEV * n_dev
@@ -52,10 +52,26 @@
 
     lax.fori_loop(1, n_dev, greet, 0)
 
-    for field, ref in enumerate((melt_ref, temp_ref)):
-        for b in range(n_ry * cap):
-            d = b // cap
-            send[d * layers : (d + 1) * layers, field * cap + b % cap, :] = ref[b]
+    loads = [pltpu.make_async_copy(ref, held.at[i], in_sem.at[i]) for i, ref in enumerate((melt_ref, temp_ref))]
+    for load in loads:
+        load.start()
+
+    lane8 = lax.broadcasted_iota(jnp.int32, (cap, 2 * k0), 1)
+    row8 = lax.broadcasted_iota(jnp.int32, (cap, 2 * k0), 0)
+    slot = (lane8 // (2 * cap)) & (n_ry - 1)
+    named = names_ref[...].astype(F32)
+    spread = jnp.zeros((cap, 2 * k0), F32)
+    for jj in range(n_ry):
+        spread = jnp.where(slot == (j + n_ry - jj) % n_ry, named[:, jj : jj + 1], spread)
+    line = jnp.sum(jnp.where(row8 == (lane8 & (cap - 1)), spread, 0.0), axis=0, keepdims=True)
+    line = jnp.where(line >= rows, 1e4, line)
+    t_ref[...] = jnp.broadcast_to(line, (8, 2 * k0))
+
+    for field in range(2):
+        loads[field].wait()
+        for d in range(n_ry):
+            send[d * layers : (d + 1) * layers, field * cap : (field + 1) * cap, :] = (
+                held[field, :, d * cap : (d + 1) * cap, :])
 
     @pl.when(jnp.logical_not(has_prev))
     def _():
@@ -93,7 +109,7 @@
     def brick_copy(i):
         d = (j + i) % n_ry
         return pltpu.make_async_remote_copy(
-            send.at[pl.ds(d * layers, layers)], recv.at[j], a_send.at[i], a_recv.at[j],
+            send.at[pl.ds(d * layers, layers)], recv.at[i], a_send.at[i], a_recv.at[i],
             device_id=worker(r, d), device_id_type=MESH)
 
     for i in range(1, n_ry):
@@ -105,7 +121,7 @@
 
     @pl.when(own_block)
     def _():
-        recv[j] = send[pl.ds(j * layers, layers)]
+        recv[0] = send[pl.ds(j * layers, layers)]
 
     @pl.when(jnp.logical_not(own_block))
     def _():
@@ -180,9 +196,12 @@
 
     for pair in range(n_ry // 2):
         for jj in (2 * pair, 2 * pair + 1):
-            @pl.when(jnp.logical_not(jnp.logical_and(own_block, j == jj)))
-            def _():
+            if jj:
                 brick_wait(jj)
+            else:
+                @pl.when(jnp.logical_not(own_block))
+                def _():
+                    brick_wait(0)
 
             @pl.when(has_next)
             def _():
@@ -247,9 +266,11 @@
 
     decay = -OPACITY / (layers * n_dev)
 
-    def march(half):
+    quarter = half_rows // 2
+
+    def march(half, part):
         def tile(i, c):
-            at = pl.ds(pl.multiple_of(half * half_rows + i * 8, 8), 8)
+            at = pl.ds(pl.multiple_of(half * half_rows + part * quarter + i * 8, 8), 8)
             through = total = red = green = None
             for z in range(layers):
                 s = sm[z + 1, at, :]
@@ -269,66 +290,69 @@
                 else:
                     through, total, red, green = through * kept, total + w, red + rw, green + gw
             to = pl.ds(pl.multiple_of(i * 8, 8), 8)
-            img[half, 0, to, :] = red
-            img[half, 1, to, :] = green
-            img[half, 2, to, :] = total - red
-            img[half, 3, to, :] = through
+            img[half, part, 0, to, :] = red
+            img[half, part, 1, to, :] = green
+            img[half, part, 2, to, :] = total - red
+            img[half, part, 3, to, :] = through
             return c
 
-        lax.fori_loop(0, half_rows // 8, tile, 0)
-
-    march(0)
-    core_copy = pltpu.make_async_remote_copy(
-        img.at[0], cin, c_send, c_recv, device_id=((r // 2) * 2 + 1 - core, j), device_id_type=MESH)
-    core_copy.start()
-    march(1)
-    core_copy.wait_recv()
+        lax.fori_loop(0, quarter // 8, tile, 0)
+
+    def core_copy(part):
+        return pltpu.make_async_remote_copy(
+            img.at[0, part], cin.at[part], c_send.at[part], c_recv.at[part],
+            device_id=((r // 2) * 2 + 1 - core, j), device_id_type=MESH)
 
     front = core == 0
-
-    for a in range(ROWS_DEV):
-        for low8 in range(n_low // 8):
-            at = slice(a * n_low + low8 * 8, a * n_low + low8 * 8 + 8)
-            mine = [img[1, ch, at, :] for ch in range(4)]
-            theirs = [cin[ch, at, :] for ch in range(4)]
-            ft = jnp.where(front, mine[3], theirs[3])
-            for ch in range(4):
-                f = jnp.where(front, mine[ch], theirs[ch])
-                b = jnp.where(front, theirs[ch], mine[ch])
-                value = f + ft * b if ch < 3 else ft * b
-                send2[low8 * 8 : low8 * 8 + 8, ch * ROWS_DEV + a, :] = value
-
     low_me = (r // 2) * n_ry + j
     group = (r // 2) * n_ry + (j % 2) * (n_ry // 2) + j // 2
 
-    def part_copy(i):
+    def part_copy(part, i):
         to = (low_me + i) % n_low
         return pltpu.make_async_remote_copy(
-            send2.at[to], parts.at[group], d_send.at[i], d_recv.at[group],
+            send2.at[part, to], parts.at[part, group], d_send.at[part, i], d_recv.at[part, group],
             device_id=((to // n_ry) * 2 + core, to % n_ry), device_id_type=MESH)
 
-    for i in range(1, n_low):
-        part_copy(i).start()
-    parts[group] = send2[low_me]
-
-    color, through = None, None
-    for g in range(n_low):
-        @pl.when(g != group)
-        def _():
-            pltpu.make_async_remote_copy(
-                send2.at[0], parts.at[g], d_send.at[0], d_recv.at[g],
-                device_id=(r, j), device_id_type=MESH).wait_recv()
-
-        value = parts[g]
-        c = value[: 3 * ROWS_DEV]
-        t = value[3 * ROWS_DEV :]
-        if g == 0:
-            color, through = c, t
-        else:
-            color = color + jnp.concatenate([through] * 3, axis=0) * c
-            through = through * t
-    out_ref[: 3 * ROWS_DEV] = color
-    out_ref[3 * ROWS_DEV :] = through
+    for part in range(2):
+        march(0, part)
+        core_copy(part).start()
+        march(1, part)
+        core_copy(part).wait_recv()
+        for a in range(2):
+            for low8 in range(n_low // 8):
+                at = slice(a * n_low + low8 * 8, a * n_low + low8 * 8 + 8)
+                mine = [img[1, part, ch, at, :] for ch in range(4)]
+                theirs = [cin[part, ch, at, :] for ch in range(4)]
+                ft = jnp.where(front, mine[3], theirs[3])
+                for ch in range(4):
+                    f = jnp.where(front, mine[ch], theirs[ch])
+                    b = jnp.where(front, theirs[ch], mine[ch])
+                    value = f + ft * b if ch < 3 else ft * b
+                    send2[part, low8 * 8 : low8 * 8 + 8, ch * 2 + a, :] = value
+        for i in range(1, n_low):
+            part_copy(part, i).start()
+        parts[part, group] = send2[part, low_me]
+
+    for part in range(2):
+        color, through = None, None
+        for g in range(n_low):
+            @pl.when(g != group)
+            def _():
+                pltpu.make_async_remote_copy(
+                    send2.at[part, 0], parts.at[part, g], d_send.at[part, 0], d_recv.at[part, g],
+                    device_id=(r, j), device_id_type=MESH).wait_recv()
+
+            value = parts[part, g]
+            t = jnp.concatenate([value[6:8]] * 4, axis=0)
+            if g == 0:
+                color, through = value, t
+            else:
+                color = color + through * value
+                through = through * t
+        for a in range(2):
+            for ch in range(4):
+                at = ch * 2 + a
+                out_ref[ch, part * 2 + a] = (color if ch < 3 else through)[at : at + 1]
 
     @pl.when(me < n_dev - 1)
     def _():
@@ -354,9 +378,10 @@
         def _():
             after_copy(jj).wait_send()
 
-    core_copy.wait_send()
-    for i in range(1, n_low):
-        part_copy(i).wait_send()
+    for part in range(2):
+        core_copy(part).wait_send()
+        for i in range(1, n_low):
+            part_copy(part, i).wait_send()
 
 
 def shards(liquid_share, thermal_field, destination_slab_line):
@@ -366,19 +391,17 @@
     n_dev = n_rx * n_ry
     rows = ROWS_DEV * n_dev
     k0 = n_ry * 2 * cap
-    lines = destination_slab_line.reshape(n_ry, 1, cap).astype(F32)
-    lines = jnp.where(lines >= rows, 1e4, lines)
-    lines = jnp.broadcast_to(lines, (n_ry, 2, cap)).reshape(1, k0)
-    lines = jnp.broadcast_to(jnp.concatenate([lines, lines], axis=1), (8, 2 * k0))
     dma = pltpu.SemaphoreType.DMA
     vmem = pltpu.VMEM
     half_rows, n_low = rows // 2, n_dev // 2
     image = pl.pallas_call(
         functools.partial(kernel, n_rx, n_ry, cap, layers, width),
-        out_shape=jax.ShapeDtypeStruct((4 * ROWS_DEV, width), F32),
-        in_specs=[pl.BlockSpec(memory_space=pltpu.VMEM)] * 3,
+        out_shape=jax.ShapeDtypeStruct((4, ROWS_DEV, 1, width), F32),
+        in_specs=[pl.BlockSpec(memory_space=pl.ANY)] * 2 + [pl.BlockSpec(memory_space=pltpu.VMEM)],
         out_specs=pl.BlockSpec(memory_space=pltpu.VMEM),
         scratch_shapes=[
+            vmem((2, layers, bricks, width), F32),
+            vmem((8, 2 * k0), F32),
             vmem((n_ry * layers, 2 * cap, width), F32),
             vmem((n_ry, layers, 2 * cap, width), F32),
             vmem((n_ry, 2, 2 * cap, width), F32),
@@ -394,21 +417,26 @@
             vmem((layers, rows, width), F32),
             vmem((layers, rows, width), F32),
             vmem((layers, rows, width), F32),
-            vmem((2, 4, half_rows, width), F32),
-            vmem((4, half_rows, width), F32),
-            vmem((n_low, 4 * ROWS_DEV, width), F32),
-            vmem((n_low, 4 * ROWS_DEV, width), F32),
+            vmem((2, 2, 4, half_rows // 2, width), F32),
+            vmem((2, 4, half_rows // 2, width), F32),
+            vmem((2, n_low, 2 * ROWS_DEV, width), F32),
+            vmem((2, n_low, 2 * ROWS_DEV, width), F32),
             dma((n_ry,)), dma((n_ry,)),
             dma((n_ry,)), dma((n_ry,)),
             dma((n_ry,)), dma((n_ry,)),
             dma((3,)), dma((3,)),
-            dma, dma,
-            dma((n_low,)), dma((n_low,)),
+            dma((2,)), dma((2,)),
+            dma((2, n_low)), dma((2, n_low)),
+            dma((2,)),
         ],
         compiler_params=pltpu.CompilerParams(
             collective_id=0, has_side_effects=True, vmem_limit_bytes=60 * 1024 * 1024),
-    )(liquid_share, thermal_field, lines)
-    return image.reshape(4, ROWS_DEV, 1, width)
+    )(
+        jnp.transpose(liquid_share, (1, 0, 2)),
+        jnp.transpose(thermal_field, (1, 0, 2)),
+        jnp.transpose(destination_slab_line[0]),
+    )
+    return image
 
 
 def solution(mesh):

time: 60.6 us -> 54.1 us (0.89); the launches traced: 59.6 us -> 53.9 us
  local copies, waits for them, and re-layouts: 5.49 us -> 1.41 us
  Pallas kernels: 53.3 us -> 52.5 us
  other arithmetic: 0.76 us -> 0 us
    unnamed x4 -> x1, local copies, waits for them, and re-layouts: 3.27 us -> 1.41 us
    reshape x2 -> x0, local copies, waits for them, and re-layouts: 1.53 us -> none  [the longest x1 1.43 us: shards(): return image.reshape(4, ROWS_DEV, 1, width)]
    pallas_call x1, Pallas kernels: 53.3 us -> 52.5 us  [shards(): pl.pallas_call(functools.partial(kernel, n_rx, n_ry, cap, layers, width),...]
    select_n x1 -> x0, other arithmetic: 0.68 us -> none  [shards(): lines = jnp.where(lines >= rows, 10000.0, lines)]
    broadcast_in_dim x2 -> x0, local copies, waits for them, and re-layouts: 0.61 us -> none  [the longest x1 0.6 us: shards(): jnp.broadcast_to(jnp.concatenate([lines, lines], axis=1), (8, 2 * k0))]
where the time goes in v2:
time: 54.1 us; the launch traced here: 53.9 us
  Pallas kernels  52.5 us (97%)
  local copies, waits for them, and re-layouts  1.41 us (3%)
    pallas_call x1, Pallas kernels, shards(): pl.pallas_call(functools.partial(kernel, n_rx, n_ry, cap, layers, width),...  52.5 us
    unnamed x1, local copies, waits for them, and re-layouts  1.41 us

profile of v2, /device:TPU:0, one launch (start us, length us, event | category | flops | bytes accessed | tf_op | source)
XLA Modules:
  0.0 53.9 jit_solution(3193627423188625944)
XLA Ops:
  0.0 52.5 %shard_map.37 = f32[4,4,1,640]{3,2,1,0:T(1,128)} custom-call(f32[5,32,640]{2,1,0:T(8,128)} %bitcast.5, f32[5,32,640]{2,1,0:T(8,128)} %bitcast.6, s32[4,8]{1,0:T(4,128)} %bitcast.7), custom_call_target="tpu_custom_call" | custom-call | tf_op jit(solution)/shard_map/pallas_call | solution.py:397
  52.5 1.4 %copy.5 = f32[4,4,1,640]{3,2,1,0:T(1,128)} copy(f32[4,4,1,640]{3,2,1,0:T(1,128)} %shard_map.37) | data formatting | bytes 81920

commit v3 on v2

--- a/solution.py
+++ b/solution.py
@@ -73,6 +73,9 @@
             send[d * layers : (d + 1) * layers, field * cap : (field + 1) * cap, :] = (
                 held[field, :, d * cap : (d + 1) * cap, :])
 
+    before[:, 0, cap : 2 * cap, :] = jnp.zeros((n_ry, cap, width), F32)
+    after[:, 1, cap : 2 * cap, :] = jnp.zeros((n_ry, cap, width), F32)
+
     @pl.when(jnp.logical_not(has_prev))
     def _():
         before[...] = jnp.zeros_like(before)
@@ -179,15 +182,27 @@
     def rows_of(ref, pair, layer):
         return ref[2 * pair : 2 * pair + 2, layer].reshape(4 * cap, width)
 
+    class Both:
+        def __init__(self, copies):
+            self.start = lambda: [c.start() for c in copies]
+            self.wait_recv = lambda: [c.wait_recv() for c in copies]
+            self.wait_send = lambda: [c.wait_send() for c in copies]
+
+    def halo(jj, ref, near, far, near_at, far_at, sends, recvs, target):
+        return Both([
+            pltpu.make_async_remote_copy(
+                recv.at[jj, near], ref.at[jj, near_at], sends.at[0, jj], recvs.at[0, jj],
+                device_id=target, device_id_type=MESH),
+            pltpu.make_async_remote_copy(
+                recv.at[jj, far, pl.ds(0, cap)], ref.at[jj, far_at, pl.ds(0, cap)], sends.at[1, jj], recvs.at[1, jj],
+                device_id=target, device_id_type=MESH),
+        ])
+
     def before_copy(jj):
-        return pltpu.make_async_remote_copy(
-            recv.at[jj, pl.ds(layers - 2, 2)], before.at[jj], hp_send.at[jj], hp_recv.at[jj],
-            device_id=worker_of((slab + 1) % n_dev), device_id_type=MESH)
+        return halo(jj, before, layers - 1, layers - 2, 1, 0, hp_send, hp_recv, worker_of((slab + 1) % n_dev))
 
     def after_copy(jj):
-        return pltpu.make_async_remote_copy(
-            recv.at[jj, pl.ds(0, 2)], after.at[jj], hn_send.at[jj], hn_recv.at[jj],
-            device_id=worker_of((slab + n_dev - 1) % n_dev), device_id_type=MESH)
+        return halo(jj, after, 0, 1, 0, 1, hn_send, hn_recv, worker_of((slab + n_dev - 1) % n_dev))
 
     def brick_wait(jj):
         pltpu.make_async_remote_copy(
@@ -422,8 +437,8 @@
             vmem((2, n_low, 2 * ROWS_DEV, width), F32),
             vmem((2, n_low, 2 * ROWS_DEV, width), F32),
             dma((n_ry,)), dma((n_ry,)),
-            dma((n_ry,)), dma((n_ry,)),
-            dma((n_ry,)), dma((n_ry,)),
+            dma((2, n_ry)), dma((2, n_ry)),
+            dma((2, n_ry)), dma((2, n_ry)),
             dma((3,)), dma((3,)),
             dma((2,)), dma((2,)),
             dma((2, n_low)), dma((2, n_low)),

time: 54.1 us -> 53.5 us (0.989)
  Pallas kernels: 52.5 us -> 51.9 us
    pallas_call x1, Pallas kernels: 52.5 us -> 51.9 us  [shards(): pl.pallas_call(functools.partial(kernel, n_rx, n_ry, cap, layers, width),...]
where the time goes in v3:
time: 53.5 us; the launch traced here: 53.3 us
  Pallas kernels  51.9 us (97%)
  local copies, waits for them, and re-layouts  1.41 us (3%)
    pallas_call x1, Pallas kernels, shards(): pl.pallas_call(functools.partial(kernel, n_rx, n_ry, cap, layers, width),...  51.9 us
    unnamed x1, local copies, waits for them, and re-layouts  1.41 us

profile of v3, /device:TPU:0, one launch (start us, length us, event | category | flops | bytes accessed | tf_op | source)
XLA Modules:
  0.0 53.3 jit_solution(10828959136414006427)
XLA Ops:
  0.0 51.9 %shard_map.37 = f32[4,4,1,640]{3,2,1,0:T(1,128)} custom-call(f32[5,32,640]{2,1,0:T(8,128)} %bitcast.5, f32[5,32,640]{2,1,0:T(8,128)} %bitcast.6, s32[4,8]{1,0:T(4,128)} %bitcast.7), custom_call_target="tpu_custom_call" | custom-call | tf_op jit(solution)/shard_map/pallas_call | solution.py:412
  51.9 1.4 %copy.5 = f32[4,4,1,640]{3,2,1,0:T(1,128)} copy(f32[4,4,1,640]{3,2,1,0:T(1,128)} %shard_map.37) | data formatting | bytes 81920

commit v4 on v3

--- a/solution.py
+++ b/solution.py
@@ -19,9 +19,9 @@
     melt_ref, temp_ref, names_ref, out_ref,
     held, t_ref, send, recv, before, after, lines,
     rhs_b, rhs_d, rhs_e, rhs_p, rhs_n, weights,
-    sm, st, gy, gx, img, cin, send2, parts,
+    sm, st, gy, gx, img, cin, img2, cin2, send2, parts,
     a_send, a_recv, hp_send, hp_recv, hn_send, hn_recv, t_send, t_recv,
-    c_send, c_recv, d_send, d_recv, in_sem,
+    c_send, c_recv, d_send, d_recv, e_send, e_recv, in_sem,
 ):
     n_dev = n_rx * n_ry
     rows = ROWS_DEV * n_dev
@@ -31,6 +31,8 @@
     r, j = lax.axis_index("rx"), lax.axis_index("ry")
     me = r * n_ry + j
     core = r % 2
+    bit1 = (j // 2) % 2
+    n_rest = n_low // 2
 
     def worker(rr, dd):
         return ((rr // 2) * 2 + dd % 2, (dd // 2) * 2 + rr % 2)
@@ -143,9 +145,13 @@
     log_ry, log_low = n_ry.bit_length() - 1, n_low.bit_length() - 1
     other_half = jnp.where(p < half_rows, 1, 0)
     side = jnp.where(other_half == 1, 1 - core, core)
-    part_a = (p >> log_low) & (ROWS_DEV - 1)
-    low = p & (n_low - 1)
-    k = ((low >> log_ry) << (log_ry + 1)) + side * n_ry + (low & (n_ry - 1))
+    log_rest = log_low - 1
+    rest = p & (n_rest - 1)
+    part_a = ((p >> (log_rest + 2)) & 1) * 2 + ((p >> log_rest) & 1)
+    side2 = jnp.where(((p >> (log_rest + 1)) & 1) == 0, 1 - bit1, bit1)
+    j_low = rest & (n_ry // 2 - 1)
+    k_j = ((j_low >> 1) << 2) + side2 * 2 + (j_low & 1)
+    k = ((rest >> (log_ry - 1)) << (log_ry + 1)) + side * n_ry + k_j
     q = (part_a * n_dev + k).astype(F32)
     is_melt = (lane & cap) == 0
 
@@ -318,39 +324,66 @@
             img.at[0, part], cin.at[part], c_send.at[part], c_recv.at[part],
             device_id=((r // 2) * 2 + 1 - core, j), device_id_type=MESH)
 
-    front = core == 0
-    low_me = (r // 2) * n_ry + j
-    group = (r // 2) * n_ry + (j % 2) * (n_ry // 2) + j // 2
+    rest_me = (r // 2) * (n_ry // 2) + (j // 4) * 2 + j % 2
+    group = (r // 2) * (n_ry // 2) + (j % 2) * (n_ry // 4) + j // 4
+
+    def chip_copy(part):
+        return pltpu.make_async_remote_copy(
+            img2.at[part, 0], cin2.at[part], e_send.at[part], e_recv.at[part],
+            device_id=(r, j + 2 - 4 * bit1), device_id_type=MESH)
 
     def part_copy(part, i):
-        to = (low_me + i) % n_low
+        to = (rest_me + i) % n_rest
+        to_j = to % (n_ry // 2)
         return pltpu.make_async_remote_copy(
             send2.at[part, to], parts.at[part, group], d_send.at[part, i], d_recv.at[part, group],
-            device_id=((to // n_ry) * 2 + core, to % n_ry), device_id_type=MESH)
-
-    for part in range(2):
-        march(0, part)
-        core_copy(part).start()
-        march(1, part)
+            device_id=((to // (n_ry // 2)) * 2 + core, (to_j // 2) * 4 + bit1 * 2 + to_j % 2), device_id_type=MESH)
+
+    def over(front, mine, theirs):
+        ft = jnp.where(front, mine[3], theirs[3])
+        for ch in range(4):
+            f = jnp.where(front, mine[ch], theirs[ch])
+            b = jnp.where(front, theirs[ch], mine[ch])
+            yield f + ft * b if ch < 3 else ft * b
+
+    def finish_core(part):
         core_copy(part).wait_recv()
-        for a in range(2):
-            for low8 in range(n_low // 8):
-                at = slice(a * n_low + low8 * 8, a * n_low + low8 * 8 + 8)
+        for h in range(2):
+            for first in range(0, n_low, 8):
+                at = slice(h * n_low + first, h * n_low + first + 8)
                 mine = [img[1, part, ch, at, :] for ch in range(4)]
                 theirs = [cin[part, ch, at, :] for ch in range(4)]
-                ft = jnp.where(front, mine[3], theirs[3])
-                for ch in range(4):
-                    f = jnp.where(front, mine[ch], theirs[ch])
-                    b = jnp.where(front, theirs[ch], mine[ch])
-                    value = f + ft * b if ch < 3 else ft * b
-                    send2[part, low8 * 8 : low8 * 8 + 8, ch * 2 + a, :] = value
-        for i in range(1, n_low):
+                for ch, value in enumerate(over(core == 0, mine, theirs)):
+                    img2[part, h, ch, first : first + 8, :] = value
+        chip_copy(part).start()
+
+    def finish_chip(part):
+        chip_copy(part).wait_recv()
+        for a in range(2):
+            for first in range(0, n_rest, 8):
+                at = slice(a * n_rest + first, a * n_rest + first + 8)
+                mine = [img2[part, 1, ch, at, :] for ch in range(4)]
+                theirs = [cin2[part, ch, at, :] for ch in range(4)]
+                for ch, value in enumerate(over(bit1 == 0, mine, theirs)):
+                    send2[part, first : first + 8, ch * 2 + a, :] = value
+        for i in range(1, n_rest):
             part_copy(part, i).start()
-        parts[part, group] = send2[part, low_me]
+        parts[part, group] = send2[part, rest_me]
+
+    march(0, 0)
+    core_copy(0).start()
+    march(1, 0)
+    finish_core(0)
+    march(0, 1)
+    core_copy(1).start()
+    march(1, 1)
+    finish_core(1)
+    finish_chip(0)
+    finish_chip(1)
 
     for part in range(2):
         color, through = None, None
-        for g in range(n_low):
+        for g in range(n_rest):
             @pl.when(g != group)
             def _():
                 pltpu.make_async_remote_copy(
@@ -395,7 +428,8 @@
 
     for part in range(2):
         core_copy(part).wait_send()
-        for i in range(1, n_low):
+        chip_copy(part).wait_send()
+        for i in range(1, n_rest):
             part_copy(part, i).wait_send()
 
 
@@ -434,14 +468,17 @@
             vmem((layers, rows, width), F32),
             vmem((2, 2, 4, half_rows // 2, width), F32),
             vmem((2, 4, half_rows // 2, width), F32),
-            vmem((2, n_low, 2 * ROWS_DEV, width), F32),
-            vmem((2, n_low, 2 * ROWS_DEV, width), F32),
+            vmem((2, 2, 4, half_rows // 4, width), F32),
+            vmem((2, 4, half_rows // 4, width), F32),
+            vmem((2, n_low // 2, 2 * ROWS_DEV, width), F32),
+            vmem((2, n_low // 2, 2 * ROWS_DEV, width), F32),
             dma((n_ry,)), dma((n_ry,)),
             dma((2, n_ry)), dma((2, n_ry)),
             dma((2, n_ry)), dma((2, n_ry)),
             dma((3,)), dma((3,)),
             dma((2,)), dma((2,)),
             dma((2, n_low)), dma((2, n_low)),
+            dma((2,)), dma((2,)),
             dma((2,)),
         ],
         compiler_params=pltpu.CompilerParams(

time: 53.5 us -> 53.7 us (level); the launches traced: 53.3 us -> 52.7 us
  Pallas kernels: 51.9 us -> 51.2 us
    pallas_call x1, Pallas kernels: 51.9 us -> 51.2 us  [shards(): pl.pallas_call(functools.partial(kernel, n_rx, n_ry, cap, layers, width),...]
where the time goes in v4:
time: 53.7 us; the launch traced here: 52.7 us
  Pallas kernels  51.2 us (95%)
  local copies, waits for them, and re-layouts  1.41 us (3%)
    pallas_call x1, Pallas kernels, shards(): pl.pallas_call(functools.partial(kernel, n_rx, n_ry, cap, layers, width),...  51.2 us
    unnamed x1, local copies, waits for them, and re-layouts  1.41 us

profile of v4, /device:TPU:0, one launch (start us, length us, event | category | flops | bytes accessed | tf_op | source)
XLA Modules:
  0.0 52.7 jit_solution(6325809140818065683)
XLA Ops:
  0.0 51.2 %shard_map.37 = f32[4,4,1,640]{3,2,1,0:T(1,128)} custom-call(f32[5,32,640]{2,1,0:T(8,128)} %bitcast.5, f32[5,32,640]{2,1,0:T(8,128)} %bitcast.6, s32[4,8]{1,0:T(4,128)} %bitcast.7), custom_call_target="tpu_custom_call" | custom-call | tf_op jit(solution)/shard_map/pallas_call | solution.py:446
  51.3 1.4 %copy.5 = f32[4,4,1,640]{3,2,1,0:T(1,128)} copy(f32[4,4,1,640]{3,2,1,0:T(1,128)} %shard_map.37) | data formatting | bytes 81920
